TPU v7x, 32 devices: a whole 2x2x4 slice. The times are simulated.
32 devices in a mesh: grp: 2 (over x), ctx: 8 (over z, y), head: 2 (over core).
Axes of the slice: x: 2, y: 2, z: 4, core: 2. Of those that a mesh axis runs over, the one named last changes fastest.
Arguments:
- cache_keys: bfloat16 [16, 8, 2048, 128], P('grp', 'head', 'ctx'), parts along dimension 0, may hold values from -4 to 4
- cache_values: bfloat16 [16, 8, 2048, 128], P('grp', 'head', 'ctx'), parts along dimension 0, may hold values from -8 to 8
- ref_queries: bfloat16 [16, 8, 256, 128], P('grp', 'head'), parts along dimension 0, may hold values from -264 to 264
- listed: int32 [16, 8, 128], P('grp', 'head'), parts along dimension 0, may hold values from 0 to 2047, as said below
Outputs:
- compact_keys: bfloat16 [16, 8, 128, 128], P('grp', 'head'), parts along dimension 0
- compact_values: bfloat16 [16, 8, 128, 128], P('grp', 'head'), parts along dimension 0
There are 2 independent parts, one for each index of `grp`. A program takes and returns all parts, laid end to end along the dimension named above; each array names one. Nothing has to cross between parts.
Inputs may be any that keep to these rules, and one draw needn't show every extreme that they name: `listed`: for each layer and head the 128 positions are distinct; at most 16 of them lie in one aligned block of 256 positions, and exactly 16 in some block.
All inputs are finite; a program needn't handle non-finite values.
Results may differ from a plain program's by a relative error of at most 0.0046.
Values may be sent and summed in bfloat16 or wider, within the bound.
A program may use at most 64 MiB of HBM per device.

v0:
```python
import math

import jax
import jax.numpy as jnp
from jax import lax
from jax.sharding import PartitionSpec as P

ridge_share = 0.05


def ridge_solve(fit_weights, moments):
    keep_count = fit_weights.shape[2]
    gram_matrix = jnp.einsum(
        "iqm,iqn->imn", fit_weights, fit_weights, precision=lax.Precision.HIGHEST
    )
    ridge_term = ridge_share * jnp.trace(gram_matrix, axis1=1, axis2=2) / keep_count
    system = gram_matrix + ridge_term[:, None, None] * jnp.eye(keep_count, dtype=jnp.float32)[None]
    factor = jnp.linalg.cholesky(system)
    halfway = lax.linalg.triangular_solve(factor, moments, left_side=True, lower=True)
    solved = lax.linalg.triangular_solve(
        factor, halfway, left_side=True, lower=True, transpose_a=True
    )
    return solved.astype(jnp.bfloat16)


def shards(cache_keys, cache_values, ref_queries, listed):
    layer_count, head_count, tok_local, head_size = cache_keys.shape
    query_count = ref_queries.shape[2]
    keep_count = listed.shape[2]
    item_count = layer_count * head_count
    shard_count = lax.axis_size("ctx")
    items_local = item_count // shard_count
    my_index = lax.axis_index("ctx")
    first_item = my_index * items_local
    score_scale = 1.0 / math.sqrt(head_size)
    query_rows = ref_queries.reshape(item_count, query_count, head_size)
    key_table = cache_keys.reshape(item_count, tok_local, head_size)
    value_table = cache_values.reshape(item_count, tok_local, head_size)
    positions = listed.reshape(item_count, keep_count)
    scores = (
        jnp.einsum("iqd,itd->iqt", query_rows, key_table, preferred_element_type=jnp.float32)
        * score_scale
    )
    row_peak = lax.pmax(jnp.max(scores, axis=-1), "ctx")
    expw = jnp.exp(scores - row_peak[:, :, None])
    totals = jnp.sum(expw, axis=-1)
    weighted = jnp.einsum(
        "iqt,itd->iqd", expw.astype(jnp.bfloat16), value_table, preferred_element_type=jnp.float32
    )
    local_pos = positions - my_index * tok_local
    is_local = (local_pos >= 0) & (local_pos < tok_local)
    clipped = jnp.clip(local_pos, 0, tok_local - 1)
    key_rows = jnp.take_along_axis(key_table, clipped[:, :, None], axis=1)
    mine_queries = lax.dynamic_slice_in_dim(query_rows, first_item, items_local, 0)
    mine_totals, mine_weighted = (
        lax.psum_scatter(totals, "ctx", scatter_dimension=0, tiled=True),
        lax.psum_scatter(weighted, "ctx", scatter_dimension=0, tiled=True),
    )
    target = mine_weighted / mine_totals[:, :, None]
    key_terms = jnp.where(is_local[:, :, None], key_rows, jnp.zeros_like(key_rows)).astype(
        jnp.float32
    )
    compact = lax.psum_scatter(
        key_terms.astype(jnp.bfloat16), "ctx", scatter_dimension=0, tiled=True
    )
    compact_scores = (
        jnp.einsum("iqd,imd->iqm", mine_queries, compact, preferred_element_type=jnp.float32)
        * score_scale
    )
    fit_weights = jax.nn.softmax(compact_scores, axis=-1)
    moments = jnp.einsum("iqm,iqd->imd", fit_weights, target, precision=lax.Precision.HIGHEST)
    solved = ridge_solve(fit_weights, moments)
    packed = jnp.stack([compact, solved], axis=1)
    gathered = lax.all_gather(packed, "ctx", axis=0, tiled=True)
    gathered = gathered.reshape(layer_count, head_count, 2, keep_count, head_size)
    return (gathered[:, :, 0], gathered[:, :, 1])


def solution(mesh):
    in_specs = (
        P("grp", "head", "ctx", None),
        P("grp", "head", "ctx", None),
        P("grp", "head", None, None),
        P("grp", "head", None),
    )
    out_specs = (P("grp", "head", None, None), P("grp", "head", None, None))
    return jax.shard_map(shards, mesh=mesh, in_specs=in_specs, out_specs=out_specs, check_vma=False)
```

profile of v0, /device:TPU:0, one launch (start us, length us, event | category | flops | bytes accessed | tf_op | source)
XLA Modules:
  0.0 276.8 jit_solution(3340144046232054518)
XLA Ops:
  7.2 0.9 subtract_clamp_fusion
  8.1 0.7 compare_and_fusion.1
  8.9 21.7 %gather_fusion = bf16[4096,128]{1,0:T(8,128)(2,1)S(1)} fusion(bf16[32,256,128]{2,1,0:T(8,128)(2,1)S(1)} %bitcast.37, s32[4096]{0:T(1024)S(1)} %fusion.26), kind=kCustom, calls=%fused_computation | custom fusion | bytes 2129920 | tf_op jit(solution)/shard_map/jit(take_along_axis)/gather | solution.py:53
  30.6 2.5 select_select_fusion
  33.1 6.1 %multiply_reduce_fusion = (f32[32,256]{1,0:T(8,128)S(1)}, f32[32,256,256]{1,2,0:T(8,128)}) fusion(bf16[32,256,128]{2,1,0:T(8,128)(2,1)} %bitcast.40, bf16[32,256,128]{2,1,0:T(8,128)(2,1)S(1)} %bitcast.38), kind=kOutput, calls=%fused_computation.2 | convolution fusion | flops 541057024 | bytes 12615680 | tf_op jit(solution)/shard_map/iqd,itd->iqt/dot_general | solution.py:41
  39.2 39.1 %pmax.7 = f32[32,256]{1,0:T(8,128)S(1)} all-reduce(f32[32,256]{1,0:T(8,128)S(1)} %get-tuple-element.4), channel_id=1, replica_groups=mesh['grp'=2,'ctx'=8,'head'=2] {'ctx'}, use_global_device_ids=true, to_apply=%region_7.8 | all-reduce | flops 8192 | bytes 65536 | tf_op jit(solution)/shard_map/pmax | solution.py:44
  78.2 7.8 %fusion.2 = f32[32,256,128]{2,1,0:T(8,128)} fusion(bf16[32,256,128]{2,1,0:T(8,128)(2,1)} %bitcast.42, f32[32,256,256]{1,2,0:T(8,128)} %get-tuple-element.5, f32[32,256]{1,0:T(8,128)S(1)} %pmax.7), kind=kOutput, calls=%fused_computation.5 | convolution fusion | flops 543162368 | bytes 14712832 | tf_op jit(solution)/shard_map/iqt,itd->iqd/dot_general | solution.py:47
  86.1 0.6 copy-done.5
  86.7 0.6 dynamic-slice
  87.9 4.8 %fusion = f32[32,256]{1,0:T(8,128)S(1)} fusion(f32[32,256,256]{1,2,0:T(8,128)} %get-tuple-element.5, f32[32,256]{1,0:T(8,128)S(1)} %pmax.7), kind=kLoop, calls=%fused_computation.3 | loop fusion | flops 6283264 | bytes 8454144 | tf_op jit(solution)/shard_map/reduce_sum | solution.py:46
  92.8 34.2 %all-reduce = f32[32,256]{1,0:T(8,128)S(1)} all-reduce(f32[32,256]{1,0:T(8,128)S(1)} %fusion), channel_id=4, replica_groups=mesh['grp'=2,'ctx'=8,'head'=2] {'ctx'}, use_global_device_ids=true, to_apply=%region_10.11.clone | all-reduce | flops 8192 | bytes 65536
  126.9 0.6 constant_dynamic-slice_fusion
  127.6 1.3 fusion.29
  129.0 0.9 select_reduce_fusion.1
  129.9 0.1 copy.11
  130.2 46.9 %custom-call.9 = f32[4,128,128]{2,1,0:T(8,128)S(1)} custom-call(f32[4,128,128]{2,1,0:T(8,128)S(1)} %fusion.15), custom_call_target="Cholesky" | custom-call | tf_op jit(solution)/shard_map/jit(cholesky)/cholesky | solution.py:18
  177.1 0.8 select_reduce_fusion
  178.1 39.3 %custom-call.10 = f32[4,1,128,128]{2,3,1,0:T(8,128)S(1)} custom-call(f32[4,1,128,128]{3,2,1,0:T(8,128)S(1)} %select_bitcast_fusion), custom_call_target="InvertDiagBlocksLowerTriangular" | custom-call | tf_op jit(solution)/shard_map/triangular_solve | solution.py:20
  217.4 1.9 fusion.7
  219.4 0.6 fusion.12
  220.0 0.4 fusion.6
  220.4 0.7 pad_maximum_fusion
  221.1 46.0 %all-gather.2.cloned.1.call-done = bf16[32,2,128,128]{3,2,0,1:T(8,128)(2,1)} async-done(((bf16[4,2,128,128]{3,2,0,1:T(8,128)(2,1)}), bf16[32,2,128,128]{3,2,0,1:T(8,128)(2,1)}) %all-gather.2.cloned.1.call-update) | async-done | bytes 2097168 | tf_op jit(solution)/shard_map/all_gather | solution.py:74
  267.1 3.1 %slice_bitcast_fusion = (bf16[8,4,128,128]{3,2,1,0:T(8,128)(2,1)}, bf16[8,4,128,128]{3,2,1,0:T(8,128)(2,1)}) fusion(bf16[8,4,2,128,128]{4,3,1,0,2:T(8,128)(2,1)} %bitcast.43), kind=kLoop, calls=%fused_computation.11 | loop fusion | bytes 4194304 | tf_op jit(solution)/shard_map/squeeze | solution.py:76
  (29 shorter events, 0.8 us)
Async XLA Ops:
  7.2 1.7 copy-start
  7.2 120.5 %reduce-scatter.3.cloned.1.call-start = ((), (), s32[]{:S(2)}) async-start(), calls=%async_computation.2 | async-start | bytes 1179648 | tf_op jit(solution)/shard_map/reduce_scatter | solution.py:63
  33.1 184.4 %reduce-scatter.5.cloned.1.call-start = ((), (), s32[]{:S(2)}) async-start(), calls=%async_computation.3 | async-start | bytes 4718592 | tf_op jit(solution)/shard_map/reduce_scatter | solution.py:57
  86.0 0.7 copy-start.5
  86.1 181.1 %all-gather.2.cloned.1.call-start = ((), (), s32[]{:S(2)}) async-start(), calls=%async_computation.4 | async-start | bytes 2359296 | tf_op jit(solution)/shard_map/all_gather | solution.py:74
  127.6 2.3 copy-start.2
  128.9 1.0 copy-start.3
  129.0 0.9 copy-start.4
  217.4 3.0 %copy-start.1 = (bf16[4,128,128]{2,1,0:T(8,128)(2,1)S(1)}, bf16[4,128,128]{2,1,0:T(8,128)(2,1)}, u32[]{:S(2)}) copy-start(bf16[4,128,128]{2,1,0:T(8,128)(2,1)} %reduce-scatter.3.cloned.1.call-done) | copy-start | bytes 393220
Sparse Core Ops, SparseCore 0:
  33.2 66.2 reduce-scatter.2
  103.5 87.1 reduce-scatter.4
  221.2 45.8 all-gather.1
where the time goes:
time: 277 us
  other arithmetic  97.1 us (35%)
  blocking collectives  73.2 us (26%)
  waiting for transfers between devices  46.1 us (17%)
  local copies, waits for them, and re-layouts  26.7 us (10%)
  matrix products  18.9 us (7%)
  between operations  14.6 us (5%)
    another operation x4, other arithmetic, ridge_solve(): factor = jnp.linalg.cholesky(system)  47.8 us
    all_gather x1, waiting for transfers between devices, shards(): gathered = lax.all_gather(packed, 'ctx', axis=0, tiled=True)  46 us
    another operation x3, other arithmetic, ridge_solve(): lax.linalg.triangular_solve(factor, halfway, left_side=True, lower=True,...  39.4 us
    pmax x1, blocking collectives, shards(): row_peak = lax.pmax(jnp.max(scores, axis=-1), 'ctx')  39.1 us
    unnamed x1, blocking collectives  34.2 us
    gather x1, local copies, waits for them, and re-layouts, shards(): key_rows = jnp.take_along_axis(key_table, clipped[:, :, None], axis=1)  21.7 us
    dot_general x1, matrix products, shards(): jnp.einsum('iqt,itd->iqd', expw.astype(jnp.bfloat16), value_table, prefer...  7.78 us
    dot_general x1, matrix products, shards(): jnp.einsum('iqd,itd->iqt', query_rows, key_table, preferred_element_type=...  6.07 us
  transfers between devices with their start and end apart: 3, of which 1 were waited for; matrix products, arithmetic and copies ran while one was open for 40% of the time, Pallas kernels for 0%

commit v1 on v0

v1 whole, which is shorter than its diff:
```python
import functools
import math

import jax
import jax.numpy as jnp
from jax import lax
from jax.experimental import pallas as pl
from jax.experimental.pallas import tpu as pltpu
from jax.sharding import PartitionSpec as P

ridge_share = 0.05
block_rows = 16
MESH = pl.DeviceIdType.MESH
EXACT = lax.Precision.HIGHEST
f32, bf16 = jnp.float32, jnp.bfloat16


def dot(a, b, dims, precision=None):
    return lax.dot_general(
        a, b, ((dims[:1], dims[1:]), ((), ())), precision=precision, preferred_element_type=f32
    )


def spectrum_steps(keep):
    low = 1.0 / (1.0 + keep / ridge_share)
    lows = []
    while 1.0 - low > 1e-7:
        lows.append(low)
        low = 4.0 * low / (1.0 + low) ** 2
    return lows


def kernel(
    n, keys, values, queries, listed, out_keys, out_values,
    local_pos, slot_code, rows_send, rows_recv, own_sum, own_stats,
    w1_send, w1_recv, s1_send, s1_recv, w2_send, w2_recv, s2_send, s2_recv, fit_map,
    rows_ss, rows_rs, w1_ss, w1_rs, s1_ss, s1_rs, w2_ss, w2_rs, s2_ss, s2_rs,
    kz_ss, kz_rs, ky_ss, ky_rs, vz_ss, vz_rs, vy_ss, vy_rs,
):
    items, tok, head = keys.shape
    query_count = queries.shape[1]
    keep = listed.shape[1]
    nz = n // 2
    ipl = items // n
    scale = 1.0 / math.sqrt(head)
    me = lax.axis_index("ctx")
    z, y = me // 2, lax.rem(me, 2)
    mate = 2 * z + 1 - y

    def copy(src, dst, ss, rs, to):
        return pltpu.make_async_remote_copy(
            src_ref=src, dst_ref=dst, send_sem=ss, recv_sem=rs,
            device_id={"ctx": to}, device_id_type=MESH,
        )

    def z_of(k):
        return lax.rem(z + 1 + k, nz)

    barrier = pltpu.get_barrier_semaphore()
    for d in range(1, n):
        pl.semaphore_signal(
            barrier, inc=1, device_id={"ctx": lax.rem(me + d, n)}, device_id_type=MESH
        )

    def attend(item):
        scores = dot(keys[item], queries[item], (1, 1))
        peak = jnp.max(scores, axis=0, keepdims=True)
        expw = jnp.exp((scores - peak) * scale)
        total = jnp.sum(expw, axis=0, keepdims=True)
        return dot(values[item], expw.astype(bf16), (0, 0)), peak, total

    before = jnp.where(
        lax.broadcasted_iota(jnp.int32, (keep, keep), 0)
        < lax.broadcasted_iota(jnp.int32, (keep, keep), 1), 1.0, 0.0,
    ).astype(bf16)
    pos = listed[...] - me * tok
    is_local = (pos >= 0) & (pos < tok)
    rank = dot(jnp.where(is_local, 1.0, 0.0).astype(bf16), before, (1, 0))
    local_pos[...] = pos
    slot_code[...] = jnp.where(is_local, rank, -1.0)
    slot_iota = lax.broadcasted_iota(jnp.int32, (block_rows, keep), 0).astype(f32)
    tok_iota = lax.broadcasted_iota(jnp.int32, (tok, keep), 0)

    def pick_rows(owner, _):
        for j in range(ipl):
            item = owner * ipl + j
            slots = jnp.where(slot_iota == slot_code[pl.ds(item, 1), :], 1.0, 0.0).astype(bf16)
            at = jnp.where(tok_iota == local_pos[pl.ds(item, 1), :], 1.0, 0.0).astype(bf16)
            chosen = dot(slots, at, (1, 1)).astype(bf16)
            rows_send[owner, j] = dot(chosen, keys[item], (1, 0)).astype(bf16)
        return 0

    def send_one(k):
        owner = 2 * z_of(k) + 1 - y
        for j in range(ipl):
            total_w, peak, total = attend(owner * ipl + j)
            w1_send[k, j] = total_w.astype(bf16)
            s1_send[k, 0, pl.ds(j, 1), :] = peak
            s1_send[k, 1, pl.ds(j, 1), :] = total

    def w1(k):
        return copy(w1_send.at[k], w1_recv.at[k], w1_ss.at[k], w1_rs.at[k], mate)

    def s1(k):
        return copy(s1_send.at[k], s1_recv.at[k], s1_ss.at[k], s1_rs.at[k], mate)

    def w2(k):
        to = 2 * z_of(k) + y
        return copy(w2_send.at[k], w2_recv.at[k], w2_ss.at[k], w2_rs.at[k], to)

    def s2(k):
        to = 2 * z_of(k) + y
        return copy(s2_send.at[k], s2_recv.at[k], s2_ss.at[k], s2_rs.at[k], to)

    def rows_copy(d):
        to = lax.rem(me + d, n)
        return copy(rows_send.at[to], rows_recv.at[me], rows_ss.at[d - 1], rows_rs.at[d - 1], to)

    def block(ref, owner):
        return ref.at[pl.ds(owner * ipl, ipl)]

    def to_z(ref, ss, rs, d):
        mine = block(ref, me)
        return copy(mine, mine, ss.at[d - 1], rs.at[d - 1], 2 * lax.rem(z + d, nz) + y)

    def to_mate(ref, ss, rs, d):
        part = block(ref, 2 * lax.rem(z - d + nz, nz) + y)
        return copy(part, part, ss.at[d], rs.at[d], mate)

    def each(low, high, step):
        def body(k, _):
            step(k)
            return 0

        lax.fori_loop(low, high, body, 0)

    send_one(0)
    pl.semaphore_wait(barrier, n - 1)
    w1(0).start()
    s1(0).start()

    def send_next(k):
        send_one(k)
        w1(k).start()
        s1(k).start()

    each(1, nz, send_next)
    lax.fori_loop(0, n, pick_rows, 0)
    each(1, n, lambda d: rows_copy(d).start())
    rows_recv[me] = rows_send[me]

    def keep_own(k):
        owner = 2 * z_of(k) + y
        for j in range(ipl):
            total_w, peak, total = attend(owner * ipl + j)
            own_sum[k, j] = total_w
            own_stats[k, 0, pl.ds(j, 1), :] = peak
            own_stats[k, 1, pl.ds(j, 1), :] = total

    each(0, nz, keep_own)

    each(1, n, lambda d: rows_copy(d).wait())
    shard_iota = lax.broadcasted_iota(jnp.int32, (n, keep), 0)
    row_iota = lax.broadcasted_iota(jnp.int32, (n * block_rows, keep), 0).astype(f32)
    gathered_rows = [
        rows_recv[:, j].reshape(n * block_rows, head) for j in range(ipl)
    ]
    for j in range(ipl):
        item = me * ipl + j
        where_listed = listed[pl.ds(item, 1), :]
        first = shard_iota * tok
        home = jnp.where((where_listed >= first) & (where_listed < first + tok), 1.0, 0.0)
        earlier = dot(home.astype(bf16), before, (1, 0))
        code = jnp.sum(
            home * (earlier + block_rows * shard_iota.astype(f32)), axis=0, keepdims=True
        )
        place = jnp.where(row_iota == code, 1.0, 0.0).astype(bf16)
        out_keys[item] = dot(place, gathered_rows[j], (0, 0)).astype(bf16)
    each(1, nz, lambda d: to_z(out_keys, kz_ss, kz_rs, d).start())

    diagonal = lax.broadcasted_iota(jnp.int32, (keep, keep), 0) == lax.broadcasted_iota(
        jnp.int32, (keep, keep), 1
    )
    unit = jnp.where(diagonal, 1.0, 0.0).astype(f32)
    fits, systems, inverses = [], [], []
    for j in range(ipl):
        item = me * ipl + j
        scores = dot(out_keys[item], queries[item], (1, 1))
        expw = jnp.exp((scores - jnp.max(scores, axis=0, keepdims=True)) * scale)
        fit = expw / jnp.sum(expw, axis=0, keepdims=True)
        gram = dot(fit, fit, (1, 1), EXACT)
        trace = jnp.sum(jnp.where(diagonal, gram, 0.0), keepdims=True)
        ridge = ridge_share * trace / keep
        bound = trace + ridge
        fits.append(fit)
        systems.append((gram + ridge * unit) / bound)
        inverses.append(unit / bound)
    lows = spectrum_steps(keep)
    for step, low in enumerate(lows):
        gain = 4.0 / (1.0 + low) ** 2
        for j in range(ipl):
            factor = gain * (1.0 + low) * unit - gain * systems[j]
            if step == 0:
                inverses[j] = factor * jnp.sum(
                    jnp.where(diagonal, inverses[j], 0.0), keepdims=True
                ) / keep
            else:
                inverses[j] = dot(factor, inverses[j], (1, 0), EXACT)
            if step < len(lows) - 1:
                systems[j] = dot(factor, systems[j], (1, 0), EXACT)
    for j in range(ipl):
        fit_map[j] = dot(inverses[j], fits[j], (1, 0), EXACT)

    def merged(k, j):
        peak_a, total_a = own_stats[k, 0, pl.ds(j, 1), :], own_stats[k, 1, pl.ds(j, 1), :]
        peak_b, total_b = s1_recv[k, 0, pl.ds(j, 1), :], s1_recv[k, 1, pl.ds(j, 1), :]
        peak = jnp.maximum(peak_a, peak_b)
        share_a = jnp.exp((peak_a - peak) * scale)
        share_b = jnp.exp((peak_b - peak) * scale)
        total_w = own_sum[k, j] * share_a + w1_recv[k, j].astype(f32) * share_b
        return total_w, peak, total_a * share_a + total_b * share_b

    def pass_on(k):
        w1(k).wait()
        s1(k).wait()
        for j in range(ipl):
            total_w, peak, total = merged(k, j)
            w2_send[k, j] = total_w.astype(bf16)
            s2_send[k, 0, pl.ds(j, 1), :] = peak
            s2_send[k, 1, pl.ds(j, 1), :] = total
        w2(k).start()
        s2(k).start()

    each(0, nz - 1, pass_on)
    w1(nz - 1).wait()
    s1(nz - 1).wait()

    to_mate(out_keys, ky_ss, ky_rs, 0).start()

    def keys_on(d):
        to_z(out_keys, kz_ss, kz_rs, d).wait()
        to_mate(out_keys, ky_ss, ky_rs, d).start()

    each(1, nz, keys_on)

    for j in range(ipl):
        total_w, peak, total = merged(nz - 1, j)
        own_sum[nz - 1, j] = total_w
        own_stats[nz - 1, 0, pl.ds(j, 1), :] = peak
        own_stats[nz - 1, 1, pl.ds(j, 1), :] = total

    def take_in(k):
        w2(k).wait()
        s2(k).wait()
        for j in range(ipl):
            peak_a = own_stats[nz - 1, 0, pl.ds(j, 1), :]
            peak_b = s2_recv[k, 0, pl.ds(j, 1), :]
            peak = jnp.maximum(peak_a, peak_b)
            share_a = jnp.exp((peak_a - peak) * scale)
            share_b = jnp.exp((peak_b - peak) * scale)
            own_sum[nz - 1, j] = own_sum[nz - 1, j] * share_a + w2_recv[k, j].astype(f32) * share_b
            own_stats[nz - 1, 0, pl.ds(j, 1), :] = peak
            own_stats[nz - 1, 1, pl.ds(j, 1), :] = (
                own_stats[nz - 1, 1, pl.ds(j, 1), :] * share_a
                + s2_recv[k, 1, pl.ds(j, 1), :] * share_b
            )

    each(0, nz - 1, take_in)
    for j in range(ipl):
        target = own_sum[nz - 1, j] / own_stats[nz - 1, 1, pl.ds(j, 1), :]
        out_values[me * ipl + j] = dot(fit_map[j], target, (1, 1), EXACT).astype(bf16)

    each(1, nz, lambda d: to_z(out_values, vz_ss, vz_rs, d).start())
    to_mate(out_values, vy_ss, vy_rs, 0).start()

    def values_on(d):
        to_z(out_values, vz_ss, vz_rs, d).wait()
        to_mate(out_values, vy_ss, vy_rs, d).start()

    each(1, nz, values_on)

    def finish(d):
        to_mate(out_keys, ky_ss, ky_rs, d).wait()
        to_mate(out_values, vy_ss, vy_rs, d).wait()

    each(0, nz, finish)


def shards(cache_keys, cache_values, ref_queries, listed):
    layer_count, head_count, tok, head = cache_keys.shape
    query_count, keep = ref_queries.shape[2], listed.shape[2]
    items = layer_count * head_count
    n = lax.axis_size("ctx")
    nz, ipl = n // 2, items // n
    vmem = pl.BlockSpec(memory_space=pltpu.VMEM)
    dma = pltpu.SemaphoreType.DMA
    out = jax.ShapeDtypeStruct((items, keep, head), bf16)
    sums = (ipl, head, query_count)
    stats = (2, ipl, query_count)
    scratch = [
        pltpu.VMEM((items, keep), jnp.int32),
        pltpu.VMEM((items, keep), f32),
        pltpu.VMEM((n, ipl, block_rows, head), bf16),
        pltpu.VMEM((n, ipl, block_rows, head), bf16),
        pltpu.VMEM((nz,) + sums, f32),
        pltpu.VMEM((nz,) + stats, f32),
        pltpu.VMEM((nz,) + sums, bf16),
        pltpu.VMEM((nz,) + sums, bf16),
        pltpu.VMEM((nz,) + stats, f32),
        pltpu.VMEM((nz,) + stats, f32),
        pltpu.VMEM((nz - 1,) + sums, bf16),
        pltpu.VMEM((nz - 1,) + sums, bf16),
        pltpu.VMEM((nz - 1,) + stats, f32),
        pltpu.VMEM((nz - 1,) + stats, f32),
        pltpu.VMEM((ipl, keep, query_count), f32),
    ]
    for count in (n - 1, nz, nz, nz - 1, nz - 1, nz - 1, nz, nz - 1, nz):
        scratch += [dma((count,)), dma((count,))]
    compact, solved = pl.pallas_call(
        functools.partial(kernel, n),
        out_shape=(out, out),
        in_specs=[vmem] * 4,
        out_specs=(vmem, vmem),
        scratch_shapes=scratch,
        compiler_params=pltpu.CompilerParams(
            collective_id=0, has_side_effects=True, vmem_limit_bytes=48 * 2**20
        ),
        name="compact_fit",
    )(
        cache_keys.reshape(items, tok, head),
        cache_values.reshape(items, tok, head),
        ref_queries.reshape(items, query_count, head),
        listed.reshape(items, keep),
    )
    shape = (layer_count, head_count, keep, head)
    return compact.reshape(shape), solved.reshape(shape)


def solution(mesh):
    in_specs = (
        P("grp", "head", "ctx", None),
        P("grp", "head", "ctx", None),
        P("grp", "head", None, None),
        P("grp", "head", None),
    )
    out_specs = (P("grp", "head", None, None), P("grp", "head", None, None))
    return jax.shard_map(shards, mesh=mesh, in_specs=in_specs, out_specs=out_specs, check_vma=False)
```

time: 277 us -> 93.1 us (0.34)
  other arithmetic: 97.1 us -> 0 us
  Pallas kernels: 0 us -> 88 us
  blocking collectives: 73.2 us -> 0 us
  waiting for transfers between devices: 46.1 us -> 0 us
  local copies, waits for them, and re-layouts: 26.7 us -> 4.24 us
  matrix products: 18.9 us -> 0 us
  between operations: 14.6 us -> 0.65 us
    pallas_call x0 -> x1, Pallas kernels: none -> 88 us  [shards(): pl.pallas_call(functools.partial(kernel, n), out_shape=(out, out), in_spe...]
    another operation x8 -> x0, other arithmetic: 88 us -> none  [the longest x4 47.8 us: ridge_solve(): factor = jnp.linalg.cholesky(system)]
    all_gather x1 -> x0, waiting for transfers between devices: 46 us -> none  [shards(): gathered = lax.all_gather(packed, 'ctx', axis=0, tiled=True)]
    pmax x1 -> x0, blocking collectives: 39.1 us -> none  [shards(): row_peak = lax.pmax(jnp.max(scores, axis=-1), 'ctx')]
    unnamed x1 -> x0, blocking collectives: 34.2 us -> none
    gather x1 -> x0, local copies, waits for them, and re-layouts: 21.7 us -> none  [shards(): key_rows = jnp.take_along_axis(key_table, clipped[:, :, None], axis=1)]
    dot_general x5 -> x0, matrix products: 17.9 us -> none  [the longest x1 7.78 us: shards(): jnp.einsum('iqt,itd->iqd', expw.astype(jnp.bfloat16), value_table, prefer...]
    reduce_sum x2 -> x0, other arithmetic: 4.94 us -> none  [the longest x1 4.85 us: shards(): totals = jnp.sum(expw, axis=-1)]
  transfers between devices with their start and end apart: 3 -> 0, of which waited for: 1 -> 0; matrix products, arithmetic and copies ran while one was open for 40% -> 0% of each run, Pallas kernels for 0% -> 0%
where the time goes in v1:
time: 93.1 us; the launch traced here: 92.8 us
  Pallas kernels  88 us (95%)
  local copies, waits for them, and re-layouts  4.24 us (5%)
    pallas_call x1, Pallas kernels, shards(): pl.pallas_call(functools.partial(kernel, n), out_shape=(out, out), in_spe...  88 us
    unnamed x6, local copies, waits for them, and re-layouts  4.24 us

profile of v1, /device:TPU:0, one launch (start us, length us, event | category | flops | bytes accessed | tf_op | source)
XLA Modules:
  0.0 92.8 jit_solution(3829589843692889078)
XLA Ops:
  0.6 0.0 copy-start
  0.6 1.6 %copy-done = bf16[8,4,256,128]{3,2,1,0:T(8,128)(2,1)S(1)} copy-done((bf16[8,4,256,128]{3,2,1,0:T(8,128)(2,1)S(1)}, bf16[8,4,256,128]{3,2,1,0:T(8,128)(2,1)}, u32[]{:S(2)}) %copy-start) | copy-done | bytes 2097176
  2.2 0.0 copy-start.1
  2.2 0.7 copy-done.1
  2.9 88.0 %compact_fit.1 = (bf16[32,128,128]{2,1,0:T(8,128)(2,1)S(1)}, bf16[32,128,128]{2,1,0:T(8,128)(2,1)S(1)}) custom-call(bf16[32,256,128]{2,1,0:T(8,128)(2,1)S(1)} %bitcast.6, bf16[32,256,128]{2,1,0:T(8,128)(2,1)} %bitcast.10, bf16[32,256,128]{2,1,0:T(8,128)(2,1)} %bitcast.11, s32[32,128]{1,0:T(8,128)S(1)} %bitcast.9), custom_call_target="tpu_custom_call" | custom-call | tf_op jit(solution)/shard_map/compact_fit/pallas_call | solution.py:319
  90.9 1.0 %copy.8 = bf16[8,4,128,128]{3,2,1,0:T(8,128)(2,1)} copy(bf16[8,4,128,128]{3,2,1,0:T(8,128)(2,1)S(1)} %bitcast.8) | data formatting | bytes 2097152
  91.9 1.0 %copy.9 = bf16[8,4,128,128]{3,2,1,0:T(8,128)(2,1)} copy(bf16[8,4,128,128]{3,2,1,0:T(8,128)(2,1)S(1)} %bitcast.7) | data formatting | bytes 2097152
Async XLA Ops:
  0.6 1.6 %copy-start = (bf16[8,4,256,128]{3,2,1,0:T(8,128)(2,1)S(1)}, bf16[8,4,256,128]{3,2,1,0:T(8,128)(2,1)}, u32[]{:S(2)}) copy-start(bf16[8,4,256,128]{3,2,1,0:T(8,128)(2,1)} %param.4) | copy-start | bytes 6291460
  2.2 0.7 copy-start.1

commit v2 on v1

v2 whole, which is shorter than its diff:
```python
import functools
import math

import jax
import jax.numpy as jnp
from jax import lax
from jax.experimental import pallas as pl
from jax.experimental.pallas import tpu as pltpu
from jax.sharding import PartitionSpec as P

ridge_share = 0.05
block_rows = 16
MESH = pl.DeviceIdType.MESH
EXACT = lax.Precision.HIGHEST
f32, bf16 = jnp.float32, jnp.bfloat16


def dot(a, b, dims, precision=None):
    return lax.dot_general(
        a, b, ((dims[:1], dims[1:]), ((), ())), precision=precision, preferred_element_type=f32
    )


def spectrum_steps(keep):
    low = 1.0 / (1.0 + keep / ridge_share)
    lows = []
    while 1.0 - low > 1e-7:
        lows.append(low)
        low = 4.0 * low / (1.0 + low) ** 2
    return lows


def kernel(
    n, keys, values, queries, listed, out_keys, out_values,
    local_pos, slot_code, rows_send, rows_recv, own_sum, own_stats,
    sum_send, sum_recv, stat_send, stat_recv, fit_map,
    rows_ss, rows_rs, sum_ss, sum_rs, stat_ss, stat_rs, key_ss, key_rs, val_ss, val_rs,
):
    items, tok, head = keys.shape
    keep = listed.shape[1]
    ipl = items // n
    bits = n.bit_length() - 1
    scale = 1.0 / math.sqrt(head)
    me = lax.axis_index("ctx")

    def copy(src, dst, ss, rs, to):
        return pltpu.make_async_remote_copy(
            src_ref=src, dst_ref=dst, send_sem=ss, recv_sem=rs,
            device_id={"ctx": to}, device_id_type=MESH,
        )

    def other(r):
        return sum(
            lax.rem(me // 2**b + r // 2**b, 2) * 2**b for b in range(bits)
        )

    def low_bit(r):
        return (r & -r).bit_length() - 1

    barrier = pltpu.get_barrier_semaphore()
    for d in range(1, n):
        pl.semaphore_signal(
            barrier, inc=1, device_id={"ctx": lax.rem(me + d, n)}, device_id_type=MESH
        )

    def attend(item):
        scores = dot(keys[item], queries[item], (1, 1))
        peak = jnp.max(scores, axis=0, keepdims=True)
        expw = jnp.exp((scores - peak) * scale)
        total = jnp.sum(expw, axis=0, keepdims=True)
        return dot(values[item], expw.astype(bf16), (0, 0)), peak, total

    before = jnp.where(
        lax.broadcasted_iota(jnp.int32, (keep, keep), 0)
        < lax.broadcasted_iota(jnp.int32, (keep, keep), 1), 1.0, 0.0,
    ).astype(bf16)
    pos = listed[...] - me * tok
    is_local = (pos >= 0) & (pos < tok)
    rank = dot(jnp.where(is_local, 1.0, 0.0).astype(bf16), before, (1, 0))
    local_pos[...] = pos
    slot_code[...] = jnp.where(is_local, rank, -1.0)
    slot_iota = lax.broadcasted_iota(jnp.int32, (block_rows, keep), 0).astype(f32)
    tok_iota = lax.broadcasted_iota(jnp.int32, (tok, keep), 0)

    def pick_rows(owner, _):
        for j in range(ipl):
            item = owner * ipl + j
            slots = jnp.where(slot_iota == slot_code[pl.ds(item, 1), :], 1.0, 0.0).astype(bf16)
            at = jnp.where(tok_iota == local_pos[pl.ds(item, 1), :], 1.0, 0.0).astype(bf16)
            chosen = dot(slots, at, (1, 1)).astype(bf16)
            rows_send[owner, j] = dot(chosen, keys[item], (1, 0)).astype(bf16)
        return 0

    def rows_copy(d):
        to = lax.rem(me + d, n)
        return copy(rows_send.at[to], rows_recv.at[me], rows_ss.at[d - 1], rows_rs.at[d - 1], to)

    def sum_copies(r, step):
        to = other(step)
        return (
            copy(sum_send.at[r], sum_recv.at[r], sum_ss.at[r], sum_rs.at[r], to),
            copy(stat_send.at[r], stat_recv.at[r], stat_ss.at[r], stat_rs.at[r], to),
        )

    def block_copy(ref, ss, rs, r):
        step = r & -r
        part = ref.at[pl.ds(other(r ^ step) * ipl, ipl)]
        return copy(part, part, ss.at[r], rs.at[r], other(step))

    def key_copy(r):
        return block_copy(out_keys, key_ss, key_rs, r)

    def value_copy(r):
        return block_copy(out_values, val_ss, val_rs, r)

    def each(low, high, step):
        def body(k, _):
            step(k)
            return 0

        lax.fori_loop(low, high, body, 0)

    def put_stats(ref, r, j, peak, total):
        ref[r, 0, pl.ds(j, 1), :] = peak
        ref[r, 1, pl.ds(j, 1), :] = total

    def get_stats(ref, r, j):
        return ref[r, 0, pl.ds(j, 1), :], ref[r, 1, pl.ds(j, 1), :]

    def send_group(k):
        r = n - 1 - 2 * k
        owner = other(r)
        for j in range(ipl):
            weighted, peak, total = attend(owner * ipl + j)
            sum_send[r, j] = weighted.astype(bf16)
            put_stats(stat_send, r, j, peak, total)

    def start_group(k):
        for sent in sum_copies(n - 1 - 2 * k, 1):
            sent.start()

    def send_next(k):
        send_group(k)
        start_group(k)

    def keep_group(k):
        owner = other(2 * k)
        for j in range(ipl):
            weighted, peak, total = attend(owner * ipl + j)
            own_sum[k, j] = weighted
            put_stats(own_stats, k, j, peak, total)

    def merge(r):
        sources = [r + 2**b for b in range(bits if r == 0 else low_bit(r))]
        for source in sources:
            for sent in sum_copies(source, source - r):
                sent.wait()
            if source == 1:
                for odd in range(1, n, 2):
                    key_copy(odd).start()
            for j in range(ipl):
                peak_a, total_a = get_stats(own_stats, r // 2, j)
                peak_b, total_b = get_stats(stat_recv, source, j)
                peak = jnp.maximum(peak_a, peak_b)
                share_a = jnp.exp((peak_a - peak) * scale)
                share_b = jnp.exp((peak_b - peak) * scale)
                weighted = own_sum[r // 2, j] * share_a + sum_recv[source, j].astype(f32) * share_b
                total = total_a * share_a + total_b * share_b
                if r > 0 and source == sources[-1]:
                    sum_send[r, j] = weighted.astype(bf16)
                    put_stats(stat_send, r, j, peak, total)
                else:
                    own_sum[r // 2, j] = weighted
                    put_stats(own_stats, r // 2, j, peak, total)
        if r > 0:
            for sent in sum_copies(r, r & -r):
                sent.start()

    send_group(0)
    pl.semaphore_wait(barrier, n - 1)
    start_group(0)
    each(1, n // 2, send_next)
    lax.fori_loop(0, n, pick_rows, 0)
    each(1, n, lambda d: rows_copy(d).start())
    rows_recv[me] = rows_send[me]
    each(0, n // 2, keep_group)

    evens = list(range(n - 2, 0, -2))
    early = evens[: (len(evens) + 1) // 2]
    merge(early[0])

    each(1, n, lambda d: rows_copy(d).wait())
    shard_iota = lax.broadcasted_iota(jnp.int32, (n, keep), 0)
    row_iota = lax.broadcasted_iota(jnp.int32, (n * block_rows, keep), 0).astype(f32)
    for j in range(ipl):
        item = me * ipl + j
        where_listed = listed[pl.ds(item, 1), :]
        first = shard_iota * tok
        home = jnp.where((where_listed >= first) & (where_listed < first + tok), 1.0, 0.0)
        earlier = dot(home.astype(bf16), before, (1, 0))
        code = jnp.sum(
            home * (earlier + block_rows * shard_iota.astype(f32)), axis=0, keepdims=True
        )
        place = jnp.where(row_iota == code, 1.0, 0.0).astype(bf16)
        rows = rows_recv[:, j].reshape(n * block_rows, head)
        out_keys[item] = dot(place, rows, (0, 0)).astype(bf16)
    for b in range(bits - 1, 0, -1):
        key_copy(2**b).start()
    for r in early[1:]:
        merge(r)

    diagonal = lax.broadcasted_iota(jnp.int32, (keep, keep), 0) == lax.broadcasted_iota(
        jnp.int32, (keep, keep), 1
    )
    unit = jnp.where(diagonal, 1.0, 0.0).astype(f32)
    fits, systems, inverses = [], [], []
    for j in range(ipl):
        item = me * ipl + j
        scores = dot(out_keys[item], queries[item], (1, 1))
        expw = jnp.exp((scores - jnp.max(scores, axis=0, keepdims=True)) * scale)
        fit = expw / jnp.sum(expw, axis=0, keepdims=True)
        gram = dot(fit, fit, (1, 1), EXACT)
        trace = jnp.sum(jnp.where(diagonal, gram, 0.0), keepdims=True)
        ridge = ridge_share * trace / keep
        bound = trace + ridge
        fits.append(fit)
        systems.append((gram + ridge * unit) / bound)
        inverses.append(1.0 / bound)
    lows = spectrum_steps(keep)
    for step, low in enumerate(lows):
        gain = 4.0 / (1.0 + low) ** 2
        for j in range(ipl):
            factor = gain * (1.0 + low) * unit - gain * systems[j]
            if step == 0:
                inverses[j] = factor * inverses[j]
            else:
                inverses[j] = dot(factor, inverses[j], (1, 0), EXACT)
            if step < len(lows) - 1:
                systems[j] = dot(factor, systems[j], (1, 0), EXACT)
    for j in range(ipl):
        fit_map[j] = dot(inverses[j], fits[j], (1, 0), EXACT)

    for r in evens[len(early):]:
        merge(r)

    arrivals = sorted(range(2, n, 2), key=lambda r: (bin(r).count("1"), -r))
    for r in arrivals:
        key_copy(r).wait()
        for b in range(low_bit(r) - 1, 0, -1):
            key_copy(r + 2**b).start()
    merge(0)
    for j in range(ipl):
        target = own_sum[0, j] / own_stats[0, 1, pl.ds(j, 1), :]
        out_values[me * ipl + j] = dot(fit_map[j], target, (1, 1), EXACT).astype(bf16)

    for b in range(bits - 1, -1, -1):
        value_copy(2**b).start()
    for r in arrivals:
        value_copy(r).wait()
        for b in range(low_bit(r) - 1, -1, -1):
            value_copy(r + 2**b).start()
    for r in range(1, n, 2):
        key_copy(r).wait()
        value_copy(r).wait()


def shards(cache_keys, cache_values, ref_queries, listed):
    layer_count, head_count, tok, head = cache_keys.shape
    query_count, keep = ref_queries.shape[2], listed.shape[2]
    items = layer_count * head_count
    n = lax.axis_size("ctx")
    ipl = items // n
    vmem = pl.BlockSpec(memory_space=pltpu.VMEM)
    dma = pltpu.SemaphoreType.DMA
    out = jax.ShapeDtypeStruct((items, keep, head), bf16)
    sums = (ipl, head, query_count)
    stats = (2, ipl, query_count)
    scratch = [
        pltpu.VMEM((items, keep), jnp.int32),
        pltpu.VMEM((items, keep), f32),
        pltpu.VMEM((n, ipl, block_rows, head), bf16),
        pltpu.VMEM((n, ipl, block_rows, head), bf16),
        pltpu.VMEM((n // 2,) + sums, f32),
        pltpu.VMEM((n // 2,) + stats, f32),
        pltpu.VMEM((n,) + sums, bf16),
        pltpu.VMEM((n,) + sums, bf16),
        pltpu.VMEM((n,) + stats, f32),
        pltpu.VMEM((n,) + stats, f32),
        pltpu.VMEM((ipl, keep, query_count), f32),
    ]
    scratch += [dma((n,))] * 10
    compact, solved = pl.pallas_call(
        functools.partial(kernel, n),
        out_shape=(out, out),
        in_specs=[vmem] * 4,
        out_specs=(vmem, vmem),
        scratch_shapes=scratch,
        compiler_params=pltpu.CompilerParams(
            collective_id=0, has_side_effects=True, vmem_limit_bytes=48 * 2**20
        ),
        name="compact_fit",
    )(
        cache_keys.reshape(items, tok, head),
        cache_values.reshape(items, tok, head),
        ref_queries.reshape(items, query_count, head),
        listed.reshape(items, keep),
    )
    shape = (layer_count, head_count, keep, head)
    return compact.reshape(shape), solved.reshape(shape)


def solution(mesh):
    in_specs = (
        P("grp", "head", "ctx", None),
        P("grp", "head", "ctx", None),
        P("grp", "head", None, None),
        P("grp", "head", None),
    )
    out_specs = (P("grp", "head", None, None), P("grp", "head", None, None))
    return jax.shard_map(shards, mesh=mesh, in_specs=in_specs, out_specs=out_specs, check_vma=False)
```

time: 93.1 us -> 85 us (0.913)
  Pallas kernels: 88 us -> 79.9 us
    pallas_call x1, Pallas kernels: 88 us -> 79.9 us  [shards(): pl.pallas_call(functools.partial(kernel, n), out_shape=(out, out), in_spe...]
where the time goes in v2:
time: 85 us; the launch traced here: 84.8 us
  Pallas kernels  79.9 us (94%)
  local copies, waits for them, and re-layouts  4.24 us (5%)
    pallas_call x1, Pallas kernels, shards(): pl.pallas_call(functools.partial(kernel, n), out_shape=(out, out), in_spe...  79.9 us
    unnamed x6, local copies, waits for them, and re-layouts  4.24 us

profile of v2, /device:TPU:0, one launch (start us, length us, event | category | flops | bytes accessed | tf_op | source)
XLA Modules:
  0.0 84.8 jit_solution(14417932663833474939)
XLA Ops:
  0.6 0.0 copy-start
  0.6 1.6 %copy-done = bf16[8,4,256,128]{3,2,1,0:T(8,128)(2,1)S(1)} copy-done((bf16[8,4,256,128]{3,2,1,0:T(8,128)(2,1)S(1)}, bf16[8,4,256,128]{3,2,1,0:T(8,128)(2,1)}, u32[]{:S(2)}) %copy-start) | copy-done | bytes 2097176
  2.2 0.0 copy-start.1
  2.2 0.7 copy-done.1
  2.9 79.9 %compact_fit.1 = (bf16[32,128,128]{2,1,0:T(8,128)(2,1)S(1)}, bf16[32,128,128]{2,1,0:T(8,128)(2,1)S(1)}) custom-call(bf16[32,256,128]{2,1,0:T(8,128)(2,1)S(1)} %bitcast.6, bf16[32,256,128]{2,1,0:T(8,128)(2,1)} %bitcast.10, bf16[32,256,128]{2,1,0:T(8,128)(2,1)} %bitcast.11, s32[32,128]{1,0:T(8,128)S(1)} %bitcast.9), custom_call_target="tpu_custom_call" | custom-call | tf_op jit(solution)/shard_map/compact_fit/pallas_call | solution.py:292
  82.8 1.0 %copy.8 = bf16[8,4,128,128]{3,2,1,0:T(8,128)(2,1)} copy(bf16[8,4,128,128]{3,2,1,0:T(8,128)(2,1)S(1)} %bitcast.8) | data formatting | bytes 2097152
  83.8 1.0 %copy.9 = bf16[8,4,128,128]{3,2,1,0:T(8,128)(2,1)} copy(bf16[8,4,128,128]{3,2,1,0:T(8,128)(2,1)S(1)} %bitcast.7) | data formatting | bytes 2097152
Async XLA Ops:
  0.6 1.6 %copy-start = (bf16[8,4,256,128]{3,2,1,0:T(8,128)(2,1)S(1)}, bf16[8,4,256,128]{3,2,1,0:T(8,128)(2,1)}, u32[]{:S(2)}) copy-start(bf16[8,4,256,128]{3,2,1,0:T(8,128)(2,1)} %param.4) | copy-start | bytes 6291460
  2.2 0.7 copy-start.1

commit v3 on v2

--- a/solution.py
+++ b/solution.py
@@ -180,14 +180,14 @@
     pl.semaphore_wait(barrier, n - 1)
     start_group(0)
     each(1, n // 2, send_next)
+    each(0, n // 2, keep_group)
+    evens = list(range(n - 2, 0, -2))
+    merge(evens[0])
     lax.fori_loop(0, n, pick_rows, 0)
     each(1, n, lambda d: rows_copy(d).start())
     rows_recv[me] = rows_send[me]
-    each(0, n // 2, keep_group)
-
-    evens = list(range(n - 2, 0, -2))
-    early = evens[: (len(evens) + 1) // 2]
-    merge(early[0])
+    for r in evens[1:]:
+        merge(r)
 
     each(1, n, lambda d: rows_copy(d).wait())
     shard_iota = lax.broadcasted_iota(jnp.int32, (n, keep), 0)
@@ -206,14 +206,12 @@
         out_keys[item] = dot(place, rows, (0, 0)).astype(bf16)
     for b in range(bits - 1, 0, -1):
         key_copy(2**b).start()
-    for r in early[1:]:
-        merge(r)
 
     diagonal = lax.broadcasted_iota(jnp.int32, (keep, keep), 0) == lax.broadcasted_iota(
         jnp.int32, (keep, keep), 1
     )
     unit = jnp.where(diagonal, 1.0, 0.0).astype(f32)
-    fits, systems, inverses = [], [], []
+    fits, pairs = [], []
     for j in range(ipl):
         item = me * ipl + j
         scores = dot(out_keys[item], queries[item], (1, 1))
@@ -224,24 +222,21 @@
         ridge = ridge_share * trace / keep
         bound = trace + ridge
         fits.append(fit)
-        systems.append((gram + ridge * unit) / bound)
-        inverses.append(1.0 / bound)
+        system = (gram + ridge * unit) / bound
+        pairs.append((system, unit / bound))
     lows = spectrum_steps(keep)
     for step, low in enumerate(lows):
         gain = 4.0 / (1.0 + low) ** 2
         for j in range(ipl):
-            factor = gain * (1.0 + low) * unit - gain * systems[j]
-            if step == 0:
-                inverses[j] = factor * inverses[j]
+            system, inverse = pairs[j]
+            factor = gain * (1.0 + low) * unit - gain * system
+            if step == len(lows) - 1:
+                fit_map[j] = dot(factor, dot(inverse, fits[j], (1, 0), EXACT), (1, 0), EXACT)
             else:
-                inverses[j] = dot(factor, inverses[j], (1, 0), EXACT)
-            if step < len(lows) - 1:
-                systems[j] = dot(factor, systems[j], (1, 0), EXACT)
-    for j in range(ipl):
-        fit_map[j] = dot(inverses[j], fits[j], (1, 0), EXACT)
-
-    for r in evens[len(early):]:
-        merge(r)
+                both = dot(
+                    factor, jnp.concatenate([system, inverse], axis=1), (1, 0), EXACT
+                )
+                pairs[j] = (both[:, :keep], both[:, keep:])
 
     arrivals = sorted(range(2, n, 2), key=lambda r: (bin(r).count("1"), -r))
     for r in arrivals:

time: 85 us -> 77.7 us (0.914)
  Pallas kernels: 79.9 us -> 72.6 us
    pallas_call x1, Pallas kernels: 79.9 us -> 72.6 us  [shards(): pl.pallas_call(functools.partial(kernel, n), out_shape=(out, out), in_spe...]
where the time goes in v3:
time: 77.7 us; the launch traced here: 77.5 us
  Pallas kernels  72.6 us (93%)
  local copies, waits for them, and re-layouts  4.24 us (5%)
    pallas_call x1, Pallas kernels, shards(): pl.pallas_call(functools.partial(kernel, n), out_shape=(out, out), in_spe...  72.6 us
    unnamed x6, local copies, waits for them, and re-layouts  4.24 us

profile of v3, /device:TPU:0, one launch (start us, length us, event | category | flops | bytes accessed | tf_op | source)
XLA Modules:
  0.0 77.5 jit_solution(9399791176003788359)
XLA Ops:
  0.6 0.0 copy-start
  0.6 1.6 %copy-done = bf16[8,4,256,128]{3,2,1,0:T(8,128)(2,1)S(1)} copy-done((bf16[8,4,256,128]{3,2,1,0:T(8,128)(2,1)S(1)}, bf16[8,4,256,128]{3,2,1,0:T(8,128)(2,1)}, u32[]{:S(2)}) %copy-start) | copy-done | bytes 2097176
  2.2 0.0 copy-start.1
  2.2 0.7 copy-done.1
  2.9 72.6 %compact_fit.1 = (bf16[32,128,128]{2,1,0:T(8,128)(2,1)S(1)}, bf16[32,128,128]{2,1,0:T(8,128)(2,1)S(1)}) custom-call(bf16[32,256,128]{2,1,0:T(8,128)(2,1)S(1)} %bitcast.6, bf16[32,256,128]{2,1,0:T(8,128)(2,1)} %bitcast.10, bf16[32,256,128]{2,1,0:T(8,128)(2,1)} %bitcast.11, s32[32,128]{1,0:T(8,128)S(1)} %bitcast.9), custom_call_target="tpu_custom_call" | custom-call | tf_op jit(solution)/shard_map/compact_fit/pallas_call | solution.py:287
  75.5 1.0 %copy.8 = bf16[8,4,128,128]{3,2,1,0:T(8,128)(2,1)} copy(bf16[8,4,128,128]{3,2,1,0:T(8,128)(2,1)S(1)} %bitcast.8) | data formatting | bytes 2097152
  76.5 1.0 %copy.9 = bf16[8,4,128,128]{3,2,1,0:T(8,128)(2,1)} copy(bf16[8,4,128,128]{3,2,1,0:T(8,128)(2,1)S(1)} %bitcast.7) | data formatting | bytes 2097152
Async XLA Ops:
  0.6 1.6 %copy-start = (bf16[8,4,256,128]{3,2,1,0:T(8,128)(2,1)S(1)}, bf16[8,4,256,128]{3,2,1,0:T(8,128)(2,1)}, u32[]{:S(2)}) copy-start(bf16[8,4,256,128]{3,2,1,0:T(8,128)(2,1)} %param.4) | copy-start | bytes 6291460
  2.2 0.7 copy-start.1

commit v4 on v3

--- a/solution.py
+++ b/solution.py
@@ -19,6 +19,23 @@
     return lax.dot_general(
         a, b, ((dims[:1], dims[1:]), ((), ())), precision=precision, preferred_element_type=f32
     )
+
+
+def split(x):
+    first = x.astype(bf16)
+    rest = x - first.astype(f32)
+    second = rest.astype(bf16)
+    return first, second, (rest - second.astype(f32)).astype(bf16)
+
+
+def product(a, b):
+    a1, a2, a3 = split(a)
+    b1, b2, b3 = split(b)
+    a12 = jnp.concatenate([a1, a2], axis=1)
+    a13 = jnp.concatenate([a1, a3], axis=1)
+    low = dot(a13, jnp.concatenate([b3, b1], axis=0), (1, 0))
+    low += dot(a12, jnp.concatenate([b2, b2], axis=0), (1, 0))
+    return low + dot(a12, jnp.concatenate([b1, b1], axis=0), (1, 0))
 
 
 def spectrum_steps(keep):
@@ -40,7 +57,7 @@
     keep = listed.shape[1]
     ipl = items // n
     bits = n.bit_length() - 1
-    scale = 1.0 / math.sqrt(head)
+    scale = math.log2(math.e) / math.sqrt(head)
     me = lax.axis_index("ctx")
 
     def copy(src, dst, ss, rs, to):
@@ -66,7 +83,7 @@
     def attend(item):
         scores = dot(keys[item], queries[item], (1, 1))
         peak = jnp.max(scores, axis=0, keepdims=True)
-        expw = jnp.exp((scores - peak) * scale)
+        expw = jnp.exp2((scores - peak) * scale)
         total = jnp.sum(expw, axis=0, keepdims=True)
         return dot(values[item], expw.astype(bf16), (0, 0)), peak, total
 
@@ -162,8 +179,8 @@
                 peak_a, total_a = get_stats(own_stats, r // 2, j)
                 peak_b, total_b = get_stats(stat_recv, source, j)
                 peak = jnp.maximum(peak_a, peak_b)
-                share_a = jnp.exp((peak_a - peak) * scale)
-                share_b = jnp.exp((peak_b - peak) * scale)
+                share_a = jnp.exp2((peak_a - peak) * scale)
+                share_b = jnp.exp2((peak_b - peak) * scale)
                 weighted = own_sum[r // 2, j] * share_a + sum_recv[source, j].astype(f32) * share_b
                 total = total_a * share_a + total_b * share_b
                 if r > 0 and source == sources[-1]:
@@ -215,7 +232,7 @@
     for j in range(ipl):
         item = me * ipl + j
         scores = dot(out_keys[item], queries[item], (1, 1))
-        expw = jnp.exp((scores - jnp.max(scores, axis=0, keepdims=True)) * scale)
+        expw = jnp.exp2((scores - jnp.max(scores, axis=0, keepdims=True)) * scale)
         fit = expw / jnp.sum(expw, axis=0, keepdims=True)
         gram = dot(fit, fit, (1, 1), EXACT)
         trace = jnp.sum(jnp.where(diagonal, gram, 0.0), keepdims=True)
@@ -231,11 +248,9 @@
             system, inverse = pairs[j]
             factor = gain * (1.0 + low) * unit - gain * system
             if step == len(lows) - 1:
-                fit_map[j] = dot(factor, dot(inverse, fits[j], (1, 0), EXACT), (1, 0), EXACT)
+                fit_map[j] = product(factor, product(inverse, fits[j]))
             else:
-                both = dot(
-                    factor, jnp.concatenate([system, inverse], axis=1), (1, 0), EXACT
-                )
+                both = product(factor, jnp.concatenate([system, inverse], axis=1))
                 pairs[j] = (both[:, :keep], both[:, keep:])
 
     arrivals = sorted(range(2, n, 2), key=lambda r: (bin(r).count("1"), -r))

time: 77.7 us -> 77.6 us (level)
  no operation moved by 1% of the time
where the time goes in v4:
time: 77.6 us; the launch traced here: 77.3 us
  Pallas kernels  72.4 us (93%)
  local copies, waits for them, and re-layouts  4.24 us (5%)
    pallas_call x1, Pallas kernels, shards(): pl.pallas_call(functools.partial(kernel, n), out_shape=(out, out), in_spe...  72.4 us
    unnamed x6, local copies, waits for them, and re-layouts  4.24 us

profile of v4, /device:TPU:0, one launch (start us, length us, event | category | flops | bytes accessed | tf_op | source)
XLA Modules:
  0.0 77.3 jit_solution(14144724827721386648)
XLA Ops:
  0.6 0.0 copy-start
  0.6 1.6 %copy-done = bf16[8,4,256,128]{3,2,1,0:T(8,128)(2,1)S(1)} copy-done((bf16[8,4,256,128]{3,2,1,0:T(8,128)(2,1)S(1)}, bf16[8,4,256,128]{3,2,1,0:T(8,128)(2,1)}, u32[]{:S(2)}) %copy-start) | copy-done | bytes 2097176
  2.2 0.0 copy-start.1
  2.2 0.7 copy-done.1
  2.9 72.4 %compact_fit.1 = (bf16[32,128,128]{2,1,0:T(8,128)(2,1)S(1)}, bf16[32,128,128]{2,1,0:T(8,128)(2,1)S(1)}) custom-call(bf16[32,256,128]{2,1,0:T(8,128)(2,1)S(1)} %bitcast.6, bf16[32,256,128]{2,1,0:T(8,128)(2,1)} %bitcast.10, bf16[32,256,128]{2,1,0:T(8,128)(2,1)} %bitcast.11, s32[32,128]{1,0:T(8,128)S(1)} %bitcast.9), custom_call_target="tpu_custom_call" | custom-call | tf_op jit(solution)/shard_map/compact_fit/pallas_call | solution.py:302
  75.4 1.0 %copy.8 = bf16[8,4,128,128]{3,2,1,0:T(8,128)(2,1)} copy(bf16[8,4,128,128]{3,2,1,0:T(8,128)(2,1)S(1)} %bitcast.8) | data formatting | bytes 2097152
  76.4 1.0 %copy.9 = bf16[8,4,128,128]{3,2,1,0:T(8,128)(2,1)} copy(bf16[8,4,128,128]{3,2,1,0:T(8,128)(2,1)S(1)} %bitcast.7) | data formatting | bytes 2097152
Async XLA Ops:
  0.6 1.6 %copy-start = (bf16[8,4,256,128]{3,2,1,0:T(8,128)(2,1)S(1)}, bf16[8,4,256,128]{3,2,1,0:T(8,128)(2,1)}, u32[]{:S(2)}) copy-start(bf16[8,4,256,128]{3,2,1,0:T(8,128)(2,1)} %param.4) | copy-start | bytes 6291460
  2.2 0.7 copy-start.1

commit v5 on v4

--- a/solution.py
+++ b/solution.py
@@ -119,16 +119,47 @@
             copy(stat_send.at[r], stat_recv.at[r], stat_ss.at[r], stat_rs.at[r], to),
         )
 
-    def block_copy(ref, ss, rs, r):
-        step = r & -r
+    value_order = list(range(bits - 1, -1, -1))
+    key_order = value_order[:-2] + value_order[-2:][::-1]
+
+    def last_bit(r, order):
+        return [b for b in order if r >> b & 1][-1]
+
+    def block_copy(ref, ss, rs, r, order):
+        step = 2 ** last_bit(r, order)
         part = ref.at[pl.ds(other(r ^ step) * ipl, ipl)]
         return copy(part, part, ss.at[r], rs.at[r], other(step))
 
     def key_copy(r):
-        return block_copy(out_keys, key_ss, key_rs, r)
+        return block_copy(out_keys, key_ss, key_rs, r, key_order)
 
     def value_copy(r):
-        return block_copy(out_values, val_ss, val_rs, r)
+        return block_copy(out_values, val_ss, val_rs, r, value_order)
+
+    def own_on(move, order):
+        for b in order:
+            move(2**b).start()
+
+    def arrivals(order):
+        blocks = sorted(
+            range(1, n),
+            key=lambda r: (bin(r).count("1"), [order.index(b) for b in order if r >> b & 1]),
+        )
+        return [
+            (r, [r + 2**b for b in order[order.index(last_bit(r, order)) + 1 :]]) for r in blocks
+        ]
+
+    def pass_on(move, order):
+        for r, later in arrivals(order):
+            if later:
+                move(r).wait()
+                for block in later:
+                    move(block).start()
+
+    def finish(move, order):
+        for r, later in arrivals(order):
+            if not later:
+                move(r).wait()
 
     def each(low, high, step):
         def body(k, _):
@@ -172,9 +203,6 @@
         for source in sources:
             for sent in sum_copies(source, source - r):
                 sent.wait()
-            if source == 1:
-                for odd in range(1, n, 2):
-                    key_copy(odd).start()
             for j in range(ipl):
                 peak_a, total_a = get_stats(own_stats, r // 2, j)
                 peak_b, total_b = get_stats(stat_recv, source, j)
@@ -221,8 +249,7 @@
         place = jnp.where(row_iota == code, 1.0, 0.0).astype(bf16)
         rows = rows_recv[:, j].reshape(n * block_rows, head)
         out_keys[item] = dot(place, rows, (0, 0)).astype(bf16)
-    for b in range(bits - 1, 0, -1):
-        key_copy(2**b).start()
+    own_on(key_copy, key_order)
 
     diagonal = lax.broadcasted_iota(jnp.int32, (keep, keep), 0) == lax.broadcasted_iota(
         jnp.int32, (keep, keep), 1
@@ -253,25 +280,16 @@
                 both = product(factor, jnp.concatenate([system, inverse], axis=1))
                 pairs[j] = (both[:, :keep], both[:, keep:])
 
-    arrivals = sorted(range(2, n, 2), key=lambda r: (bin(r).count("1"), -r))
-    for r in arrivals:
-        key_copy(r).wait()
-        for b in range(low_bit(r) - 1, 0, -1):
-            key_copy(r + 2**b).start()
+    pass_on(key_copy, key_order)
     merge(0)
     for j in range(ipl):
         target = own_sum[0, j] / own_stats[0, 1, pl.ds(j, 1), :]
         out_values[me * ipl + j] = dot(fit_map[j], target, (1, 1), EXACT).astype(bf16)
 
-    for b in range(bits - 1, -1, -1):
-        value_copy(2**b).start()
-    for r in arrivals:
-        value_copy(r).wait()
-        for b in range(low_bit(r) - 1, -1, -1):
-            value_copy(r + 2**b).start()
-    for r in range(1, n, 2):
-        key_copy(r).wait()
-        value_copy(r).wait()
+    own_on(value_copy, value_order)
+    pass_on(value_copy, value_order)
+    finish(key_copy, key_order)
+    finish(value_copy, value_order)
 
 
 def shards(cache_keys, cache_values, ref_queries, listed):

time: 77.6 us -> 72.8 us (0.938)
  Pallas kernels: 72.4 us -> 67.7 us
    pallas_call x1, Pallas kernels: 72.4 us -> 67.7 us  [shards(): pl.pallas_call(functools.partial(kernel, n), out_shape=(out, out), in_spe...]
where the time goes in v5:
time: 72.8 us; the launch traced here: 72.6 us
  Pallas kernels  67.7 us (93%)
  local copies, waits for them, and re-layouts  4.24 us (6%)
    pallas_call x1, Pallas kernels, shards(): pl.pallas_call(functools.partial(kernel, n), out_shape=(out, out), in_spe...  67.7 us
    unnamed x6, local copies, waits for them, and re-layouts  4.24 us

profile of v5, /device:TPU:0, one launch (start us, length us, event | category | flops | bytes accessed | tf_op | source)
XLA Modules:
  0.0 72.6 jit_solution(8001489474223124102)
XLA Ops:
  0.6 0.0 copy-start
  0.6 1.6 %copy-done = bf16[8,4,256,128]{3,2,1,0:T(8,128)(2,1)S(1)} copy-done((bf16[8,4,256,128]{3,2,1,0:T(8,128)(2,1)S(1)}, bf16[8,4,256,128]{3,2,1,0:T(8,128)(2,1)}, u32[]{:S(2)}) %copy-start) | copy-done | bytes 2097176
  2.2 0.0 copy-start.1
  2.2 0.7 copy-done.1
  2.9 67.7 %compact_fit.1 = (bf16[32,128,128]{2,1,0:T(8,128)(2,1)S(1)}, bf16[32,128,128]{2,1,0:T(8,128)(2,1)S(1)}) custom-call(bf16[32,256,128]{2,1,0:T(8,128)(2,1)S(1)} %bitcast.6, bf16[32,256,128]{2,1,0:T(8,128)(2,1)} %bitcast.10, bf16[32,256,128]{2,1,0:T(8,128)(2,1)} %bitcast.11, s32[32,128]{1,0:T(8,128)S(1)} %bitcast.9), custom_call_target="tpu_custom_call" | custom-call | tf_op jit(solution)/shard_map/compact_fit/pallas_call | solution.py:320
  70.7 1.0 %copy.8 = bf16[8,4,128,128]{3,2,1,0:T(8,128)(2,1)} copy(bf16[8,4,128,128]{3,2,1,0:T(8,128)(2,1)S(1)} %bitcast.8) | data formatting | bytes 2097152
  71.6 1.0 %copy.9 = bf16[8,4,128,128]{3,2,1,0:T(8,128)(2,1)} copy(bf16[8,4,128,128]{3,2,1,0:T(8,128)(2,1)S(1)} %bitcast.7) | data formatting | bytes 2097152
Async XLA Ops:
  0.6 1.6 %copy-start = (bf16[8,4,256,128]{3,2,1,0:T(8,128)(2,1)S(1)}, bf16[8,4,256,128]{3,2,1,0:T(8,128)(2,1)}, u32[]{:S(2)}) copy-start(bf16[8,4,256,128]{3,2,1,0:T(8,128)(2,1)} %param.4) | copy-start | bytes 6291460
  2.2 0.7 copy-start.1

commit v6 on v5

--- a/solution.py
+++ b/solution.py
@@ -48,10 +48,11 @@
 
 
 def kernel(
-    n, keys, values, queries, listed, out_keys, out_values,
-    local_pos, slot_code, rows_send, rows_recv, own_sum, own_stats,
+    n, all_keys, all_values, all_queries, listed, out_keys, out_values,
+    keys, values, queries,    local_pos, slot_code, rows_send, rows_recv, own_sum, own_stats,
     sum_send, sum_recv, stat_send, stat_recv, fit_map,
     rows_ss, rows_rs, sum_ss, sum_rs, stat_ss, stat_rs, key_ss, key_rs, val_ss, val_rs,
+    load_sems,
 ):
     items, tok, head = keys.shape
     keep = listed.shape[1]
@@ -79,6 +80,25 @@
         pl.semaphore_signal(
             barrier, inc=1, device_id={"ctx": lax.rem(me + d, n)}, device_id_type=MESH
         )
+
+    def loads(r):
+        part = pl.ds(other(r) * ipl, ipl)
+        pairs = ((all_keys, keys), (all_queries, queries), (all_values, values))
+        return [
+            pltpu.make_async_copy(source.at[part], held.at[part], load_sems.at[i, r])
+            for i, (source, held) in enumerate(pairs)
+        ]
+
+    def start_loads(r):
+        for load in loads(r):
+            load.start()
+
+    def wait_loads(r):
+        for load in loads(r):
+            load.wait()
+
+    for r in list(range(n - 1, 0, -2)) + list(range(0, n, 2)):
+        start_loads(r)
 
     def attend(item):
         scores = dot(keys[item], queries[item], (1, 1))
@@ -178,6 +198,7 @@
     def send_group(k):
         r = n - 1 - 2 * k
         owner = other(r)
+        wait_loads(r)
         for j in range(ipl):
             weighted, peak, total = attend(owner * ipl + j)
             sum_send[r, j] = weighted.astype(bf16)
@@ -193,6 +214,7 @@
 
     def keep_group(k):
         owner = other(2 * k)
+        wait_loads(2 * k)
         for j in range(ipl):
             weighted, peak, total = attend(owner * ipl + j)
             own_sum[k, j] = weighted
@@ -303,7 +325,12 @@
     out = jax.ShapeDtypeStruct((items, keep, head), bf16)
     sums = (ipl, head, query_count)
     stats = (2, ipl, query_count)
-    scratch = [
+    held = [
+        pltpu.VMEM((items, tok, head), bf16),
+        pltpu.VMEM((items, tok, head), bf16),
+        pltpu.VMEM((items, query_count, head), bf16),
+    ]
+    scratch = held + [
         pltpu.VMEM((items, keep), jnp.int32),
         pltpu.VMEM((items, keep), f32),
         pltpu.VMEM((n, ipl, block_rows, head), bf16),
@@ -316,11 +343,11 @@
         pltpu.VMEM((n,) + stats, f32),
         pltpu.VMEM((ipl, keep, query_count), f32),
     ]
-    scratch += [dma((n,))] * 10
+    scratch += [dma((n,))] * 10 + [dma((3, n))]
     compact, solved = pl.pallas_call(
         functools.partial(kernel, n),
         out_shape=(out, out),
-        in_specs=[vmem] * 4,
+        in_specs=[pl.BlockSpec(memory_space=pl.ANY)] * 3 + [vmem],
         out_specs=(vmem, vmem),
         scratch_shapes=scratch,
         compiler_params=pltpu.CompilerParams(

time: 72.8 us -> 71 us (0.975)
  Pallas kernels: 67.7 us -> 65.8 us
    pallas_call x1, Pallas kernels: 67.7 us -> 65.8 us  [shards(): pl.pallas_call(functools.partial(kernel, n), out_shape=(out, out), in_spe...]
where the time goes in v6:
time: 71 us; the launch traced here: 70.7 us
  Pallas kernels  65.8 us (93%)
  local copies, waits for them, and re-layouts  4.24 us (6%)
    pallas_call x1, Pallas kernels, shards(): pl.pallas_call(functools.partial(kernel, n), out_shape=(out, out), in_spe...  65.8 us
    unnamed x6, local copies, waits for them, and re-layouts  4.24 us

profile of v6, /device:TPU:0, one launch (start us, length us, event | category | flops | bytes accessed | tf_op | source)
XLA Modules:
  0.0 70.7 jit_solution(14497175014742708839)
XLA Ops:
  0.6 0.0 copy-start
  0.6 1.6 %copy-done = bf16[8,4,256,128]{3,2,1,0:T(8,128)(2,1)S(1)} copy-done((bf16[8,4,256,128]{3,2,1,0:T(8,128)(2,1)S(1)}, bf16[8,4,256,128]{3,2,1,0:T(8,128)(2,1)}, u32[]{:S(2)}) %copy-start) | copy-done | bytes 2097176
  2.2 0.0 copy-start.1
  2.2 0.7 %copy-done.1 = s32[8,4,128]{2,1,0:T(4,128)S(1)} copy-done((s32[8,4,128]{2,1,0:T(4,128)S(1)}, s32[8,4,128]{2,1,0:T(4,128)}, u32[]{:S(2)}) %copy-start.1) | copy-done | bytes 16408
  2.9 65.8 %compact_fit.1 = (bf16[32,128,128]{2,1,0:T(8,128)(2,1)S(1)}, bf16[32,128,128]{2,1,0:T(8,128)(2,1)S(1)}) custom-call(bf16[32,256,128]{2,1,0:T(8,128)(2,1)S(1)} %bitcast.6, bf16[32,256,128]{2,1,0:T(8,128)(2,1)} %bitcast.10, bf16[32,256,128]{2,1,0:T(8,128)(2,1)} %bitcast.11, s32[32,128]{1,0:T(8,128)S(1)} %bitcast.9), custom_call_target="tpu_custom_call" | custom-call | tf_op jit(solution)/shard_map/compact_fit/pallas_call | solution.py:347
  68.8 1.0 %copy.8 = bf16[8,4,128,128]{3,2,1,0:T(8,128)(2,1)} copy(bf16[8,4,128,128]{3,2,1,0:T(8,128)(2,1)S(1)} %bitcast.8) | data formatting | bytes 2097152
  69.8 1.0 %copy.9 = bf16[8,4,128,128]{3,2,1,0:T(8,128)(2,1)} copy(bf16[8,4,128,128]{3,2,1,0:T(8,128)(2,1)S(1)} %bitcast.7) | data formatting | bytes 2097152
Async XLA Ops:
  0.6 1.6 %copy-start = (bf16[8,4,256,128]{3,2,1,0:T(8,128)(2,1)S(1)}, bf16[8,4,256,128]{3,2,1,0:T(8,128)(2,1)}, u32[]{:S(2)}) copy-start(bf16[8,4,256,128]{3,2,1,0:T(8,128)(2,1)} %param.4) | copy-start | bytes 6291460
  2.2 0.7 %copy-start.1 = (s32[8,4,128]{2,1,0:T(4,128)S(1)}, s32[8,4,128]{2,1,0:T(4,128)}, u32[]{:S(2)}) copy-start(s32[8,4,128]{2,1,0:T(4,128)} %param.7) | copy-start | bytes 49156
